TPU v7x, 32 devices: a whole 2x2x4 slice. The times are simulated.
32 devices in a mesh: groups: 2 (over y), dp: 8 (over z, x), tensor: 2 (over core).
Axes of the slice: x: 2, y: 2, z: 4, core: 2. Of those that a mesh axis runs over, the one named last changes fastest.
Arguments:
- tokens_in: bfloat16 [2048, 4096], P(('groups', 'dp'), 'tensor'), parts along dimension 0, may hold values from -6 to 6
- grads_out: bfloat16 [2048, 12288], P(('groups', 'dp'), 'tensor'), parts along dimension 0, may hold values from -6 to 6
- proj_in: bfloat16 [4096, 64], P('tensor'), may hold values from -0.09375 to 0.09375
- proj_out: bfloat16 [12288, 64], P('tensor'), may hold values from -0.0546875 to 0.0546875
- lengths: int32 [16, 32], P('groups'), parts along dimension 0, may hold values from 1 to 64, 128 in all within a row
- train_feats: bfloat16 [6144, 4096], P(('groups', 'dp'), 'tensor'), parts along dimension 0, may hold values from -0.09375 to 0.09375
Outputs:
- scores: bfloat16 [512, 3072], P(('groups', 'tensor'), 'dp'), parts along dimension 0
There are 2 independent parts, one for each index of `groups`. A program takes and returns all parts, laid end to end along the dimension named above; an argument that names none is the same for every part. Nothing has to cross between parts.
Inputs may be any that keep to these rules, and one draw needn't show every extreme that they name: Each row of 32 lengths sums to 128, and some example in each row has exactly 64 tokens.
All inputs are finite; a program needn't handle non-finite values.
Results may differ from a plain program's by a relative error of at most 0.0049.
Values may be sent and summed in bfloat16 or wider, within the bound.
A program may use at most 128 MiB of HBM per device.

v0:
```python
import jax
import jax.numpy as jnp
from jax import lax
from jax.sharding import PartitionSpec as P


def score_rows(query_rows, train_feats):
    return lax.dot_general(
        query_rows, train_feats, (((1,), (1,)), ((), ())), preferred_element_type=jnp.float32
    )


def member_table(block_lengths, tok_count):
    stop_at = jnp.cumsum(block_lengths, axis=1)
    start_at = stop_at - block_lengths
    position = jnp.arange(tok_count, dtype=jnp.int32)
    return (
        (position[None, None, :] >= start_at[:, :, None])
        & (position[None, None, :] < stop_at[:, :, None])
    ).astype(jnp.float32)


def shards(tokens_in, grads_out, proj_in, proj_out, lengths, train_feats):
    x_part = jnp.dot(tokens_in, proj_in, preferred_element_type=jnp.float32)
    g_part = jnp.dot(grads_out, proj_out, preferred_element_type=jnp.float32)
    x_owned = lax.psum_scatter(x_part, "tensor", scatter_dimension=1, tiled=True)
    g_total = lax.psum(g_part, "tensor")
    tok_count = tokens_in.shape[0]
    own_index = lax.axis_index("dp")
    own_lengths = lax.dynamic_slice_in_dim(lengths, own_index, 1, 0)
    member = member_table(own_lengths, tok_count)[0]
    outer_rows = (x_owned[:, :, None] * g_total[:, None, :]).reshape(tok_count, -1)
    features = jnp.dot(
        member, outer_rows, precision=lax.Precision.HIGHEST, preferred_element_type=jnp.float32
    ).astype(jnp.bfloat16)
    everything = lax.all_gather(features, "dp", axis=0, tiled=True)
    partial_value = score_rows(everything, train_feats)
    return lax.psum_scatter(partial_value, "tensor", scatter_dimension=0, tiled=True).astype(
        jnp.bfloat16
    )


def solution(mesh):
    return jax.shard_map(
        shards,
        mesh=mesh,
        in_specs=(
            P(("groups", "dp"), "tensor"),
            P(("groups", "dp"), "tensor"),
            P("tensor", None),
            P("tensor", None),
            P("groups", None),
            P(("groups", "dp"), "tensor"),
        ),
        out_specs=P(("groups", "tensor"), "dp"),
        check_vma=False,
    )
```

profile of v0, /device:TPU:1, one launch (start us, length us, event | category | flops | bytes accessed | tf_op | source)
XLA Modules:
  0.0 80.6 jit_solution(2079363350432698723)
XLA Ops:
  6.5 0.0 copy-start
  6.5 0.0 reduce-scatter.3.cloned.1.call-start
  6.5 2.1 %fusion.4 = f32[128,64]{0,1:T(8,128)} fusion(bf16[128,2048]{1,0:T(8,128)(2,1)} %param.6, bf16[2048,64]{0,1:T(8,128)(2,1)} %param.8), kind=kOutput, calls=%fused_computation.9 | convolution fusion | flops 33554432 | bytes 819200 | tf_op jit(solution)/shard_map/dot_general | solution.py:24
  8.7 0.0 reduce-scatter.3.cloned.1.call-update
  8.7 0.0 all-gather.2.cloned.1.call-start
  8.8 0.7 constant_dynamic-slice_fusion
  9.5 0.2 reduce_window_sum.11
  9.7 2.3 %fusion.5 = f32[128,64]{0,1:T(8,128)S(1)} fusion(bf16[128,6144]{1,0:T(8,128)(2,1)} %param.7, bf16[6144,64]{0,1:T(8,128)(2,1)} %param.9), kind=kOutput, calls=%fused_computation.10 | convolution fusion | flops 100663296 | bytes 2392064 | tf_op jit(solution)/shard_map/dot_general | solution.py:25
  11.9 0.7 subtract_bitcast_fusion
  12.6 3.4 %psum.7 = f32[128,64]{0,1:T(8,128)S(1)} all-reduce(f32[128,64]{0,1:T(8,128)S(1)} %fusion.5), channel_id=1, replica_groups=mesh['groups'=2,'dp'=8,'tensor'=2] {'tensor'}, use_global_device_ids=true, to_apply=%region_2.0 | all-reduce | flops 8192 | bytes 65536 | tf_op jit(solution)/shard_map/psum | solution.py:27
  16.0 3.4 %reduce-scatter.3.cloned.1.call-done = f32[128,32]{0,1:T(8,128)} async-done(((f32[128,64]{0,1:T(8,128)}), f32[128,32]{0,1:T(8,128)}) %reduce-scatter.3.cloned.1.call-update) | async-done | bytes 16400 | tf_op jit(solution)/shard_map/reduce_scatter | solution.py:26
  19.4 0.8 %broadcast_multiply_fusion = f32[128,32,64]{0,2,1:T(8,128)S(1)} fusion(f32[128,64]{0,1:T(8,128)S(1)} %psum.7, f32[128,32]{0,1:T(8,128)} %reduce-scatter.3.cloned.1.call-done), kind=kLoop, calls=%fused_computation.1 | loop fusion | flops 262144 | bytes 1097728 | tf_op jit(solution)/shard_map/mul | solution.py:32
  20.3 1.3 %convolution_convert_fusion = bf16[32,2048]{1,0:T(8,128)(2,1)} fusion(f32[128,2048]{0,1:T(8,128)S(1)} %bitcast.11, s32[32]{0:T(128)S(1)} %bitcast.12, s32[32]{0:T(128)S(1)} %subtract_bitcast_fusion), kind=kOutput, calls=%fused_computation | convolution fusion | flops 100741120 | bytes 1179904 | tf_op jit(solution)/shard_map/dot_general | solution.py:33
  21.6 0.0 all-gather.2.cloned.1.call-update
  21.6 0.0 reduce-scatter.5.cloned.1.call-start
  21.7 40.1 %all-gather.2.cloned.1.call-done = bf16[256,2048]{1,0:T(8,128)(2,1)} async-done(((bf16[32,2048]{1,0:T(8,128)(2,1)}), bf16[256,2048]{1,0:T(8,128)(2,1)}) %all-gather.2.cloned.1.call-update) | async-done | bytes 1048592 | tf_op jit(solution)/shard_map/all_gather | solution.py:36
  61.8 0.0 copy-done
  61.8 2.7 %fusion.6 = f32[256,384]{1,0:T(8,128)} fusion(bf16[256,2048]{1,0:T(8,128)(2,1)} %all-gather.2.cloned.1.call-done, bf16[384,2048]{1,0:T(8,128)(2,1)S(1)} %copy-done), kind=kOutput, calls=%fused_computation.11 | convolution fusion | flops 402653184 | bytes 3014656 | tf_op jit(solution)/shard_map/dot_general | solution.py:8
  64.5 0.0 reduce-scatter.5.cloned.1.call-update
  64.5 8.0 %reduce-scatter.5.cloned.1.call-done = f32[128,384]{1,0:T(8,128)} async-done(((f32[256,384]{1,0:T(8,128)}), f32[128,384]{1,0:T(8,128)}) %reduce-scatter.5.cloned.1.call-update) | async-done | bytes 196624 | tf_op jit(solution)/shard_map/reduce_scatter | solution.py:38
  72.5 1.6 %convert_element_type.8 = bf16[128,384]{1,0:T(8,128)(2,1)} convert(f32[128,384]{1,0:T(8,128)} %reduce-scatter.5.cloned.1.call-done) | non-fusion elementwise | flops 49152 | bytes 294912 | tf_op jit(solution)/shard_map/convert_element_type | solution.py:38
Async XLA Ops:
  6.5 55.2 %copy-start = (bf16[384,2048]{1,0:T(8,128)(2,1)S(1)}, bf16[384,2048]{1,0:T(8,128)(2,1)}, u32[]{:S(2)}) copy-start(bf16[384,2048]{1,0:T(8,128)(2,1)} %param.11) | copy-start | bytes 4718596
  6.5 12.9 %reduce-scatter.3.cloned.1.call-start = ((), (), s32[]{:S(2)}) async-start(), calls=%async_computation.2 | async-start | bytes 49152 | tf_op jit(solution)/shard_map/reduce_scatter | solution.py:26
  8.7 53.1 %all-gather.2.cloned.1.call-start = ((), (), s32[]{:S(2)}) async-start(), calls=%async_computation.3 | async-start | bytes 1179648 | tf_op jit(solution)/shard_map/all_gather | solution.py:36
  21.6 50.9 %reduce-scatter.5.cloned.1.call-start = ((), (), s32[]{:S(2)}) async-start(), calls=%async_computation.4 | async-start | bytes 589824 | tf_op jit(solution)/shard_map/reduce_scatter | solution.py:38
Sparse Core Ops, SparseCore 0:
  9.5 9.8 reduce-scatter.2
  21.7 39.9 all-gather.1
  64.6 7.8 reduce-scatter.4
where the time goes:
time: 81.3 us; the launch traced here: 80.6 us
  waiting for transfers between devices  51.5 us (63%)
  between operations  13.1 us (16%)
  matrix products  8.46 us (10%)
  blocking collectives  3.39 us (4%)
  other arithmetic  3.32 us (4%)
    all_gather x1, waiting for transfers between devices, shards(): everything = lax.all_gather(features, 'dp', axis=0, tiled=True)  40.1 us
    reduce_scatter x1, waiting for transfers between devices, shards(): lax.psum_scatter(partial_value, 'tensor', scatter_dimension=0, tiled=True)  8.04 us
    psum x1, blocking collectives, shards(): g_total = lax.psum(g_part, 'tensor')  3.39 us
    reduce_scatter x1, waiting for transfers between devices, shards(): lax.psum_scatter(x_part, 'tensor', scatter_dimension=1, tiled=True)  3.37 us
    dot_general x1, matrix products, score_rows(): lax.dot_general(query_rows, train_feats, (((1,), (1,)), ((), ())), prefer...  2.7 us
    dot_general x1, matrix products, shards(): g_part = jnp.dot(grads_out, proj_out, preferred_element_type=jnp.float32)  2.28 us
    dot_general x1, matrix products, shards(): x_part = jnp.dot(tokens_in, proj_in, preferred_element_type=jnp.float32)  2.14 us
  transfers between devices with their start and end apart: 3, of which 3 were waited for; matrix products, arithmetic and copies ran while one was open for 5% of the time, Pallas kernels for 0%

commit v1 on v0

v1 whole, which is shorter than its diff:
```python
import functools

import jax
import jax.numpy as jnp
from jax import lax
from jax.experimental import pallas as pl
from jax.experimental.pallas import tpu as pltpu
from jax.sharding import PartitionSpec as P

G_PIECES = 2
GROUP = 4
F_PIECES = 8


def peer(**axes):
    return dict(device_id=axes, device_id_type=pl.DeviceIdType.MESH)


def nt(a, b):
    return lax.dot_general(a, b, (((1,), (1,)), ((), ())), preferred_element_type=jnp.float32)


def nn(a, b):
    return jnp.dot(a, b, preferred_element_type=jnp.float32)


def kernel(n_dp, tok_hbm, grd_hbm, pin_hbm, pout_hbm, len_hbm, train_hbm, out_ref,
           tok, grd, pin, pout, lens, train, part, other, xg, outer,
           load_sem, train_sem, swap_send, swap_recv, a_send, a_recv, b_send, b_recv):
    n_blocks = n_dp // 2
    group = min(GROUP, n_blocks)
    dp = lax.axis_index("dp")
    core = lax.axis_index("tensor")
    sibling = 1 - core
    owner = dp // n_blocks == core
    slot = lax.rem(dp, n_blocks)
    K, n_tok = part.shape[1:]
    n_ex = lens.shape[1]
    ff = grd.shape[1] // G_PIECES

    barrier = pltpu.get_barrier_semaphore()
    pl.semaphore_signal(barrier, inc=1, **peer(tensor=sibling))

    def greet(j, carry):
        to = core * n_blocks + j

        @pl.when(to != dp)
        def _():
            pl.semaphore_signal(barrier, inc=1, **peer(dp=to))

        return carry

    lax.fori_loop(0, n_blocks, greet, 0, unroll=n_blocks <= 8)

    loads = [
        pltpu.make_async_copy(pin_hbm, pin, load_sem.at[0]),
        pltpu.make_async_copy(tok_hbm, tok, load_sem.at[1]),
    ]
    for k in range(G_PIECES):
        cols = pl.ds(k * ff, ff)
        loads.append(pltpu.make_async_copy(pout_hbm.at[:, cols], pout.at[:, cols], load_sem.at[2 + 2 * k]))
        loads.append(pltpu.make_async_copy(grd_hbm.at[:, cols], grd.at[:, cols], load_sem.at[3 + 2 * k]))
    loads.append(pltpu.make_async_copy(len_hbm, lens, load_sem.at[2 + 2 * G_PIECES]))
    for load in loads:
        load.start()
    own_train = pltpu.make_async_copy(train_hbm, train.at[core], train_sem)
    own_train.start()

    @pl.when(owner)
    def _():
        pl.semaphore_wait(barrier, n_dp)

    @pl.when(jnp.logical_not(owner))
    def _():
        pl.semaphore_wait(barrier, 1)

    swap = pltpu.make_async_remote_copy(
        train_hbm, train.at[core], swap_send, swap_recv, **peer(tensor=sibling))
    swap.start()

    def to_owner(p):
        return pltpu.make_async_remote_copy(
            part.at[p], other.at[p], a_send.at[p], a_recv.at[p], **peer(tensor=sibling))

    def to_peer(p, k):
        return pltpu.make_async_remote_copy(
            xg.at[slot, p], xg.at[slot, p], b_send.at[p, k], b_recv.at[slot, p],
            **peer(dp=lax.rem(dp + k, n_dp)))

    def each_peer(act):
        def step(k, carry):
            act(k)
            return carry

        lax.fori_loop(1, n_dp, step, 0, unroll=n_dp <= 8)

    def hand_over(p):
        @pl.when(jnp.logical_not(owner))
        def _():
            to_owner(p).start()

    def spread(p):
        @pl.when(owner)
        def _():
            to_owner(p).wait_recv()
            xg[slot, p] = (part[p] + other[p]).astype(jnp.bfloat16)
            each_peer(lambda k: to_peer(p, k).start())

    loads[0].wait()
    loads[1].wait()
    part[0] = nt(pin[...], tok[...])
    hand_over(0)
    for k in range(G_PIECES):
        loads[2 + 2 * k].wait()
        loads[3 + 2 * k].wait()
        term = nt(pout[:, k * ff:(k + 1) * ff], grd[:, k * ff:(k + 1) * ff])
        if k == 0:
            part[1] = term
            spread(0)
        else:
            part[1] += term
    hand_over(1)
    spread(1)

    loads[-1].wait()
    q_all = group * n_ex
    k_of = lax.broadcasted_iota(jnp.int32, (n_ex, q_all), 0)
    e_of = lax.rem(lax.broadcasted_iota(jnp.int32, (n_ex, q_all), 1), n_ex)
    lens_f = lens[...].astype(jnp.float32).astype(jnp.bfloat16)
    stops = nn(lens_f, (k_of <= e_of).astype(jnp.float32).astype(jnp.bfloat16))
    starts = nn(lens_f, (k_of < e_of).astype(jnp.float32).astype(jnp.bfloat16))
    row_of = lax.broadcasted_iota(jnp.int32, (n_dp, q_all), 0)
    block_of = lax.broadcasted_iota(jnp.int32, (n_dp, q_all), 1) // n_ex
    t_of = lax.broadcasted_iota(jnp.int32, (group * n_tok, q_all), 0)
    q_of = lax.broadcasted_iota(jnp.int32, (group * n_tok, q_all), 1)
    same = t_of // n_tok == q_of // n_ex
    place = lax.rem(t_of, n_tok).astype(jnp.float32)

    def score(first, wait_train):
        mine = row_of == core * n_blocks + first + block_of
        stop = jnp.sum(jnp.where(mine, stops, 0.0), axis=0, keepdims=True)
        start = jnp.sum(jnp.where(mine, starts, 0.0), axis=0, keepdims=True)
        member = jnp.where(same & (place >= start) & (place < stop), 1.0, 0.0).astype(jnp.bfloat16)

        for j in range(group):
            at = first + j

            @pl.when(jnp.logical_not(owner & (at == slot)))
            def _():
                for p in range(2):
                    pltpu.make_async_remote_copy(
                        xg.at[at, p], xg.at[at, p], b_send.at[p, 0], b_recv.at[at, p],
                        **peer(tensor=sibling)).wait_recv()

            x = xg[at, 0].astype(jnp.float32)
            g = xg[at, 1]
            for i in range(K):
                row = jnp.broadcast_to(x[i:i + 1], (16, n_tok)).astype(jnp.bfloat16)
                outer[i * K:(i + 1) * K, j * n_tok:(j + 1) * n_tok] = (
                    jnp.concatenate([row] * (K // 16), axis=0) * g)

        wait_train()
        size = K * K // F_PIECES
        half = K * K // 2
        acc = None
        for c in range(F_PIECES):
            rows = slice(c * size, (c + 1) * size)
            f = nn(outer[rows, :], member).astype(jnp.bfloat16)
            h, at = divmod(c * size, half)
            term = nn(train[h, :, at:at + size], f)
            acc = term if acc is None else acc + term
        return acc.T.astype(out_ref.dtype)

    def train_here():
        own_train.wait()
        pltpu.make_async_remote_copy(
            train_hbm, train.at[sibling], swap_send, swap_recv, **peer(tensor=sibling)).wait_recv()

    if n_blocks == group:
        out_ref[...] = score(0, train_here)
    else:
        train_here()

        def step(s, carry):
            out_ref[pl.ds(pl.multiple_of(s * q_all, q_all), q_all), :] = score(s * group, lambda: None)
            return carry

        lax.fori_loop(0, n_blocks // group, step, 0)

    swap.wait_send()

    @pl.when(jnp.logical_not(owner))
    def _():
        for p in range(2):
            to_owner(p).wait_send()

    @pl.when(owner)
    def _():
        for p in range(2):
            each_peer(lambda k: to_peer(p, k).wait_send())


def shards(n_dp, tokens_in, grads_out, proj_in, proj_out, lengths, train_feats):
    n_tok, d = tokens_in.shape
    ff = grads_out.shape[1]
    K = proj_in.shape[1]
    n_ex = lengths.shape[1]
    n_train, half = train_feats.shape
    n_blocks = n_dp // 2
    group = min(GROUP, n_blocks)
    bf16, f32 = jnp.bfloat16, jnp.float32
    dma = pltpu.SemaphoreType.DMA
    return pl.pallas_call(
        functools.partial(kernel, n_dp),
        out_shape=jax.ShapeDtypeStruct((n_blocks * n_ex, n_train), bf16),
        in_specs=[pl.BlockSpec(memory_space=pltpu.HBM)] * 6,
        out_specs=pl.BlockSpec(memory_space=pltpu.VMEM),
        scratch_shapes=[
            pltpu.VMEM((n_tok, d), bf16),
            pltpu.VMEM((n_tok, ff), bf16),
            pltpu.VMEM((K, d), bf16),
            pltpu.VMEM((K, ff), bf16),
            pltpu.VMEM(lengths.shape, jnp.int32),
            pltpu.VMEM((2, n_train, half), bf16),
            pltpu.VMEM((2, K, n_tok), f32),
            pltpu.VMEM((2, K, n_tok), f32),
            pltpu.VMEM((n_blocks, 2, K, n_tok), bf16),
            pltpu.VMEM((K * K, group * n_tok), bf16),
            dma((3 + 2 * G_PIECES,)),
            dma,
            dma,
            dma,
            dma((2,)),
            dma((2,)),
            dma((2, n_dp)),
            dma((n_blocks, 2)),
        ],
        compiler_params=pltpu.CompilerParams(
            collective_id=0, has_side_effects=True, vmem_limit_bytes=63 * 1024 * 1024),
        cost_estimate=pl.CostEstimate(flops=10**9, bytes_accessed=5 * 10**6, transcendentals=0),
    )(tokens_in, grads_out, proj_in.T, proj_out.T, lengths, train_feats)


def solution(mesh):
    return jax.shard_map(
        functools.partial(shards, mesh.shape["dp"]),
        mesh=mesh,
        in_specs=(
            P(("groups", "dp"), "tensor"),
            P(("groups", "dp"), "tensor"),
            P("tensor", None),
            P("tensor", None),
            P("groups", None),
            P(("groups", "dp"), "tensor"),
        ),
        out_specs=P(("groups", "tensor"), "dp"),
        check_vma=False,
    )
```

time: 81.3 us -> 16.4 us (0.20)
  waiting for transfers between devices: 51.5 us -> 0 us
  Pallas kernels: 0 us -> 14.7 us
  between operations: 13.1 us -> 0.01 us
  matrix products: 8.46 us -> 0 us
  blocking collectives: 3.39 us -> 0 us
  other arithmetic: 3.32 us -> 0 us
  local copies, waits for them, and re-layouts: 0.7 us -> 1.54 us
    all_gather x1 -> x0, waiting for transfers between devices: 40.1 us -> none  [shards(): everything = lax.all_gather(features, 'dp', axis=0, tiled=True)]
    pallas_call x0 -> x1, Pallas kernels: none -> 14.7 us  [shards(): pl.pallas_call(functools.partial(kernel, n_dp), out_shape=jax.ShapeDtypeS...]
    reduce_scatter x2 -> x0, waiting for transfers between devices: 11.4 us -> none  [the longest x1 8.04 us: shards(): lax.psum_scatter(partial_value, 'tensor', scatter_dimension=0, tiled=True)]
    dot_general x4 -> x0, matrix products: 8.46 us -> none  [the longest x1 2.7 us: score_rows(): lax.dot_general(query_rows, train_feats, (((1,), (1,)), ((), ())), prefer...]
    psum x1 -> x0, blocking collectives: 3.39 us -> none  [shards(): g_total = lax.psum(g_part, 'tensor')]
    convert_element_type x1 -> x0, other arithmetic: 1.58 us -> none  [shards(): lax.psum_scatter(partial_value, 'tensor', scatter_dimension=0, tiled=True)]
    unnamed x2 -> x1, local copies, waits for them, and re-layouts: 0.01 us -> 1.54 us
    mul x1 -> x0, other arithmetic: 0.83 us -> none  [shards(): x_owned[:, :, None] * g_total[:, None, :]]
  transfers between devices with their start and end apart: 3 -> 0, of which waited for: 3 -> 0; matrix products, arithmetic and copies ran while one was open for 5% -> 0% of each run, Pallas kernels for 0% -> 0%
where the time goes in v1:
time: 16.4 us; the launch traced here: 16.2 us
  Pallas kernels  14.7 us (90%)
  local copies, waits for them, and re-layouts  1.54 us (9%)
    pallas_call x1, Pallas kernels, shards(): pl.pallas_call(functools.partial(kernel, n_dp), out_shape=jax.ShapeDtypeS...  14.7 us
    unnamed x1, local copies, waits for them, and re-layouts  1.54 us

profile of v1, /device:TPU:1, one launch (start us, length us, event | category | flops | bytes accessed | tf_op | source)
XLA Modules:
  0.0 16.2 jit_solution(5759879542064289744)
XLA Ops:
  0.0 14.7 %shard_map.64 = bf16[128,384]{1,0:T(8,128)(2,1)} custom-call(bf16[128,2048]{1,0:T(8,128)(2,1)} %tok_hbm.1, bf16[128,6144]{1,0:T(8,128)(2,1)} %grd_hbm.1, bf16[64,2048]{1,0:T(8,128)(2,1)} %bitcast.3, bf16[64,6144]{1,0:T(8,128)(2,1)} %bitcast.2, s32[8,32]{1,0:T(8,128)} %len_hbm.1, bf16[384,2048]{1,0:T(8,128)(2,1)} %train_hbm.1), custom_call_target="tpu_custom_call" | custom-call | flops 1000000000 | bytes 5000000 | tf_op jit(solution)/shard_map/pallas_call | solution.py:213
  14.7 1.5 %copy.8 = bf16[128,384]{1,0:T(8,128)(2,1)} copy(bf16[128,384]{1,0:T(8,128)(2,1)} %shard_map.64) | data formatting | bytes 196608

commit v2 on v1

--- a/solution.py
+++ b/solution.py
@@ -9,7 +9,6 @@
 
 G_PIECES = 2
 GROUP = 4
-F_PIECES = 8
 
 
 def peer(**axes):
@@ -25,7 +24,7 @@
 
 
 def kernel(n_dp, tok_hbm, grd_hbm, pin_hbm, pout_hbm, len_hbm, train_hbm, out_ref,
-           tok, grd, pin, pout, lens, train, part, other, xg, outer,
+           tok, grd, pin, pout, lens, train, part, other, xg, outer, feats,
            load_sem, train_sem, swap_send, swap_recv, a_send, a_recv, b_send, b_recv):
     n_blocks = n_dp // 2
     group = min(GROUP, n_blocks)
@@ -66,17 +65,8 @@
     own_train = pltpu.make_async_copy(train_hbm, train.at[core], train_sem)
     own_train.start()
 
-    @pl.when(owner)
-    def _():
-        pl.semaphore_wait(barrier, n_dp)
-
-    @pl.when(jnp.logical_not(owner))
-    def _():
-        pl.semaphore_wait(barrier, 1)
-
     swap = pltpu.make_async_remote_copy(
         train_hbm, train.at[core], swap_send, swap_recv, **peer(tensor=sibling))
-    swap.start()
 
     def to_owner(p):
         return pltpu.make_async_remote_copy(
@@ -97,6 +87,8 @@
     def hand_over(p):
         @pl.when(jnp.logical_not(owner))
         def _():
+            if p == 0:
+                pl.semaphore_wait(barrier, 1)
             to_owner(p).start()
 
     def spread(p):
@@ -104,6 +96,8 @@
         def _():
             to_owner(p).wait_recv()
             xg[slot, p] = (part[p] + other[p]).astype(jnp.bfloat16)
+            if p == 0:
+                pl.semaphore_wait(barrier, n_dp)
             each_peer(lambda k: to_peer(p, k).start())
 
     loads[0].wait()
@@ -116,11 +110,12 @@
         term = nt(pout[:, k * ff:(k + 1) * ff], grd[:, k * ff:(k + 1) * ff])
         if k == 0:
             part[1] = term
-            spread(0)
         else:
             part[1] += term
     hand_over(1)
+    spread(0)
     spread(1)
+    swap.start()
 
     loads[-1].wait()
     q_all = group * n_ex
@@ -131,16 +126,16 @@
     starts = nn(lens_f, (k_of < e_of).astype(jnp.float32).astype(jnp.bfloat16))
     row_of = lax.broadcasted_iota(jnp.int32, (n_dp, q_all), 0)
     block_of = lax.broadcasted_iota(jnp.int32, (n_dp, q_all), 1) // n_ex
-    t_of = lax.broadcasted_iota(jnp.int32, (group * n_tok, q_all), 0)
-    q_of = lax.broadcasted_iota(jnp.int32, (group * n_tok, q_all), 1)
-    same = t_of // n_tok == q_of // n_ex
-    place = lax.rem(t_of, n_tok).astype(jnp.float32)
+    t_of = lax.broadcasted_iota(jnp.int32, (q_all, n_tok), 1).astype(jnp.float32)
 
     def score(first, wait_train):
         mine = row_of == core * n_blocks + first + block_of
         stop = jnp.sum(jnp.where(mine, stops, 0.0), axis=0, keepdims=True)
         start = jnp.sum(jnp.where(mine, starts, 0.0), axis=0, keepdims=True)
-        member = jnp.where(same & (place >= start) & (place < stop), 1.0, 0.0).astype(jnp.bfloat16)
+        stop = jnp.broadcast_to(stop, (n_tok, q_all)).T
+        start = jnp.broadcast_to(start, (n_tok, q_all)).T
+        member = jnp.where((t_of >= start) & (t_of < stop), 1.0, 0.0).astype(jnp.bfloat16)
+        gap = jnp.zeros((n_tok, K), jnp.bfloat16)
 
         for j in range(group):
             at = first + j
@@ -153,22 +148,21 @@
                         **peer(tensor=sibling)).wait_recv()
 
             x = xg[at, 0].astype(jnp.float32)
-            g = xg[at, 1]
+            g = xg[at, 1].astype(jnp.float32).T.astype(jnp.bfloat16)
+            own = member[j * n_ex:(j + 1) * n_ex]
             for i in range(K):
                 row = jnp.broadcast_to(x[i:i + 1], (16, n_tok)).astype(jnp.bfloat16)
-                outer[i * K:(i + 1) * K, j * n_tok:(j + 1) * n_tok] = (
-                    jnp.concatenate([row] * (K // 16), axis=0) * g)
+                row = jnp.concatenate([row] * (n_ex // 16), axis=0)
+                outer[i // 2 * n_ex:(i // 2 + 1) * n_ex, i % 2 * n_tok:(i % 2 + 1) * n_tok] = row * own
+            pair = jnp.concatenate(
+                [jnp.concatenate([g, gap], axis=1), jnp.concatenate([gap, g], axis=1)], axis=0)
+            f = nn(outer[...], pair).astype(jnp.bfloat16)
+            for i in range(K // 2):
+                feats[j * n_ex:(j + 1) * n_ex, i * 2 * K:(i + 1) * 2 * K] = f[i * n_ex:(i + 1) * n_ex]
 
         wait_train()
-        size = K * K // F_PIECES
         half = K * K // 2
-        acc = None
-        for c in range(F_PIECES):
-            rows = slice(c * size, (c + 1) * size)
-            f = nn(outer[rows, :], member).astype(jnp.bfloat16)
-            h, at = divmod(c * size, half)
-            term = nn(train[h, :, at:at + size], f)
-            acc = term if acc is None else acc + term
+        acc = nt(train[0], feats[:, :half]) + nt(train[1], feats[:, half:])
         return acc.T.astype(out_ref.dtype)
 
     def train_here():
@@ -225,7 +219,8 @@
             pltpu.VMEM((2, K, n_tok), f32),
             pltpu.VMEM((2, K, n_tok), f32),
             pltpu.VMEM((n_blocks, 2, K, n_tok), bf16),
-            pltpu.VMEM((K * K, group * n_tok), bf16),
+            pltpu.VMEM((K // 2 * n_ex, 2 * n_tok), bf16),
+            pltpu.VMEM((group * n_ex, K * K), bf16),
             dma((3 + 2 * G_PIECES,)),
             dma,
             dma,
@@ -236,9 +231,9 @@
             dma((n_blocks, 2)),
         ],
         compiler_params=pltpu.CompilerParams(
-            collective_id=0, has_side_effects=True, vmem_limit_bytes=63 * 1024 * 1024),
+            collective_id=0, has_side_effects=True, vmem_limit_bytes=40 * 1024 * 1024),
         cost_estimate=pl.CostEstimate(flops=10**9, bytes_accessed=5 * 10**6, transcendentals=0),
-    )(tokens_in, grads_out, proj_in.T, proj_out.T, lengths, train_feats)
+    )(*[pltpu.with_memory_space_constraint(a, pltpu.HBM) for a in (tokens_in, grads_out, proj_in.T, proj_out.T, lengths, train_feats)])
 
 
 def solution(mesh):

time: 16.4 us -> 14 us (0.85)
  Pallas kernels: 14.7 us -> 13.2 us
  local copies, waits for them, and re-layouts: 1.54 us -> 0.64 us
    pallas_call x1, Pallas kernels: 14.7 us -> 13.2 us  [shards(): pl.pallas_call(functools.partial(kernel, n_dp), out_shape=jax.ShapeDtypeS...]
    unnamed x1, local copies, waits for them, and re-layouts: 1.54 us -> 0.64 us
where the time goes in v2:
time: 14 us; the launch traced here: 13.8 us
  Pallas kernels  13.2 us (94%)
  local copies, waits for them, and re-layouts  0.64 us (5%)
    pallas_call x1, Pallas kernels, shards(): pl.pallas_call(functools.partial(kernel, n_dp), out_shape=jax.ShapeDtypeS...  13.2 us
    unnamed x1, local copies, waits for them, and re-layouts  0.64 us

profile of v2, /device:TPU:1, one launch (start us, length us, event | category | flops | bytes accessed | tf_op | source)
XLA Modules:
  0.0 13.8 jit_solution(1467843679170069856)
XLA Ops:
  0.0 13.2 %shard_map.64 = bf16[128,384]{1,0:T(8,128)(2,1)S(1)} custom-call(bf16[128,2048]{1,0:T(8,128)(2,1)} %tok_hbm.1, bf16[128,6144]{1,0:T(8,128)(2,1)} %grd_hbm.1, bf16[64,2048]{1,0:T(8,128)(2,1)} %bitcast.3, bf16[64,6144]{1,0:T(8,128)(2,1)} %bitcast.2, s32[8,32]{1,0:T(8,128)} %len_hbm.1, bf16[384,2048]{1,0:T(8,128)(2,1)} %train_hbm.1), custom_call_target="tpu_custom_call" | custom-call | flops 1000000000 | bytes 5000000 | tf_op jit(solution)/shard_map/pallas_call | solution.py:207
  13.2 0.6 %copy.8 = bf16[128,384]{1,0:T(8,128)(2,1)} copy(bf16[128,384]{1,0:T(8,128)(2,1)S(1)} %shard_map.64) | data formatting | bytes 196608

commit v3 on v2

--- a/solution.py
+++ b/solution.py
@@ -11,6 +11,9 @@
 GROUP = 4
 
 
+ORDERS = [4, 0, 2, 6, 3, 5, 1, 7], [0, 1, 2, 3, 4, 5, 6, 7]
+
+
 def peer(**axes):
     return dict(device_id=axes, device_id_type=pl.DeviceIdType.MESH)
 
@@ -24,7 +27,7 @@
 
 
 def kernel(n_dp, tok_hbm, grd_hbm, pin_hbm, pout_hbm, len_hbm, train_hbm, out_ref,
-           tok, grd, pin, pout, lens, train, part, other, xg, outer, feats,
+           tok, grd, pin, pout, lens, train, part, other, xg, outer, member_ref, feats,
            load_sem, train_sem, swap_send, swap_recv, a_send, a_recv, b_send, b_recv):
     n_blocks = n_dp // 2
     group = min(GROUP, n_blocks)
@@ -63,7 +66,6 @@
     for load in loads:
         load.start()
     own_train = pltpu.make_async_copy(train_hbm, train.at[core], train_sem)
-    own_train.start()
 
     swap = pltpu.make_async_remote_copy(
         train_hbm, train.at[core], swap_send, swap_recv, **peer(tensor=sibling))
@@ -72,17 +74,22 @@
         return pltpu.make_async_remote_copy(
             part.at[p], other.at[p], a_send.at[p], a_recv.at[p], **peer(tensor=sibling))
 
-    def to_peer(p, k):
-        return pltpu.make_async_remote_copy(
-            xg.at[slot, p], xg.at[slot, p], b_send.at[p, k], b_recv.at[slot, p],
-            **peer(dp=lax.rem(dp + k, n_dp)))
-
     def each_peer(act):
-        def step(k, carry):
-            act(k)
-            return carry
-
-        lax.fori_loop(1, n_dp, step, 0, unroll=n_dp <= 8)
+        def one(t):
+            @pl.when(t != dp)
+            def _():
+                act(pltpu.make_async_remote_copy(
+                    xg.at[slot], xg.at[slot], b_send.at[t], b_recv.at[slot], **peer(dp=t)))
+
+        if n_dp == len(ORDERS[0]):
+            for low, high in zip(*ORDERS):
+                one(jnp.where(core == 0, low, high))
+        else:
+            def step(t, carry):
+                one(t)
+                return carry
+
+            lax.fori_loop(0, n_dp, step, 0)
 
     def hand_over(p):
         @pl.when(jnp.logical_not(owner))
@@ -91,14 +98,14 @@
                 pl.semaphore_wait(barrier, 1)
             to_owner(p).start()
 
-    def spread(p):
+    def spread():
         @pl.when(owner)
         def _():
-            to_owner(p).wait_recv()
-            xg[slot, p] = (part[p] + other[p]).astype(jnp.bfloat16)
-            if p == 0:
-                pl.semaphore_wait(barrier, n_dp)
-            each_peer(lambda k: to_peer(p, k).start())
+            for p in range(2):
+                to_owner(p).wait_recv()
+                xg[slot, p] = (part[p] + other[p]).astype(jnp.bfloat16)
+            pl.semaphore_wait(barrier, n_dp)
+            each_peer(lambda copy: copy.start())
 
     loads[0].wait()
     loads[1].wait()
@@ -113,8 +120,8 @@
         else:
             part[1] += term
     hand_over(1)
-    spread(0)
-    spread(1)
+    spread()
+    own_train.start()
     swap.start()
 
     loads[-1].wait()
@@ -135,35 +142,45 @@
         stop = jnp.broadcast_to(stop, (n_tok, q_all)).T
         start = jnp.broadcast_to(start, (n_tok, q_all)).T
         member = jnp.where((t_of >= start) & (t_of < stop), 1.0, 0.0).astype(jnp.bfloat16)
-        gap = jnp.zeros((n_tok, K), jnp.bfloat16)
-
-        for j in range(group):
-            at = first + j
-
+        gap = jnp.zeros((K, n_tok), jnp.bfloat16)
+        member_ref[...] = member
+
+        def arrive(at):
             @pl.when(jnp.logical_not(owner & (at == slot)))
             def _():
-                for p in range(2):
-                    pltpu.make_async_remote_copy(
-                        xg.at[at, p], xg.at[at, p], b_send.at[p, 0], b_recv.at[at, p],
-                        **peer(tensor=sibling)).wait_recv()
-
-            x = xg[at, 0].astype(jnp.float32)
-            g = xg[at, 1].astype(jnp.float32).T.astype(jnp.bfloat16)
-            own = member[j * n_ex:(j + 1) * n_ex]
+                pltpu.make_async_remote_copy(
+                    xg.at[at], xg.at[at], b_send.at[0], b_recv.at[at], **peer(tensor=sibling)).wait_recv()
+
+        def fill(j, buffer):
+            x = xg[first + j, 0].astype(jnp.float32)
+            g = xg[first + j, 1]
+            rows = pl.ds(pl.multiple_of(j * n_ex, n_ex), n_ex)
+            own = member_ref[rows, :]
             for i in range(K):
                 row = jnp.broadcast_to(x[i:i + 1], (16, n_tok)).astype(jnp.bfloat16)
                 row = jnp.concatenate([row] * (n_ex // 16), axis=0)
-                outer[i // 2 * n_ex:(i // 2 + 1) * n_ex, i % 2 * n_tok:(i % 2 + 1) * n_tok] = row * own
+                outer[buffer, i // 2 * n_ex:(i // 2 + 1) * n_ex, i % 2 * n_tok:(i % 2 + 1) * n_tok] = row * own
             pair = jnp.concatenate(
                 [jnp.concatenate([g, gap], axis=1), jnp.concatenate([gap, g], axis=1)], axis=0)
-            f = nn(outer[...], pair).astype(jnp.bfloat16)
+            f = nt(outer[buffer], pair).astype(jnp.bfloat16)
             for i in range(K // 2):
-                feats[j * n_ex:(j + 1) * n_ex, i * 2 * K:(i + 1) * 2 * K] = f[i * n_ex:(i + 1) * n_ex]
+                feats[rows, i * 2 * K:(i + 1) * 2 * K] = f[i * n_ex:(i + 1) * n_ex]
+
+        for j in range(0, group, 2):
+            turn = [j + k for k in range(min(2, group - j))]
+            for at in turn:
+                arrive(first + at)
+            for k, at in enumerate(turn):
+                fill(at, k)
 
         wait_train()
         half = K * K // 2
-        acc = nt(train[0], feats[:, :half]) + nt(train[1], feats[:, half:])
-        return acc.T.astype(out_ref.dtype)
+        terms = []
+        rows = train.shape[1] // 3
+        for r in range(3):
+            acc = nt(feats[:, :half], train[0, r * rows:(r + 1) * rows]) + nt(feats[:, half:], train[1, r * rows:(r + 1) * rows])
+            terms.append(acc.astype(out_ref.dtype))
+        return jnp.concatenate(terms, axis=1)
 
     def train_here():
         own_train.wait()
@@ -190,8 +207,7 @@
 
     @pl.when(owner)
     def _():
-        for p in range(2):
-            each_peer(lambda k: to_peer(p, k).wait_send())
+        each_peer(lambda copy: copy.wait_send())
 
 
 def shards(n_dp, tokens_in, grads_out, proj_in, proj_out, lengths, train_feats):
@@ -219,7 +235,8 @@
             pltpu.VMEM((2, K, n_tok), f32),
             pltpu.VMEM((2, K, n_tok), f32),
             pltpu.VMEM((n_blocks, 2, K, n_tok), bf16),
-            pltpu.VMEM((K // 2 * n_ex, 2 * n_tok), bf16),
+            pltpu.VMEM((2, K // 2 * n_ex, 2 * n_tok), bf16),
+            pltpu.VMEM((group * n_ex, n_tok), bf16),
             pltpu.VMEM((group * n_ex, K * K), bf16),
             dma((3 + 2 * G_PIECES,)),
             dma,
@@ -227,8 +244,8 @@
             dma,
             dma((2,)),
             dma((2,)),
-            dma((2, n_dp)),
-            dma((n_blocks, 2)),
+            dma((n_dp,)),
+            dma((n_blocks,)),
         ],
         compiler_params=pltpu.CompilerParams(
             collective_id=0, has_side_effects=True, vmem_limit_bytes=40 * 1024 * 1024),

time: 14 us -> 13.4 us (0.957)
  Pallas kernels: 13.2 us -> 12.6 us
    pallas_call x1, Pallas kernels: 13.2 us -> 12.6 us  [shards(): pl.pallas_call(functools.partial(kernel, n_dp), out_shape=jax.ShapeDtypeS...]
where the time goes in v3:
time: 13.4 us; the launch traced here: 13.2 us
  Pallas kernels  12.6 us (94%)
  local copies, waits for them, and re-layouts  0.64 us (5%)
    pallas_call x1, Pallas kernels, shards(): pl.pallas_call(functools.partial(kernel, n_dp), out_shape=jax.ShapeDtypeS...  12.6 us
    unnamed x1, local copies, waits for them, and re-layouts  0.64 us

profile of v3, /device:TPU:1, one launch (start us, length us, event | category | flops | bytes accessed | tf_op | source)
XLA Modules:
  0.0 13.2 jit_solution(8909242182872920565)
XLA Ops:
  0.0 12.6 %shard_map.64 = bf16[128,384]{1,0:T(8,128)(2,1)S(1)} custom-call(bf16[128,2048]{1,0:T(8,128)(2,1)} %tok_hbm.1, bf16[128,6144]{1,0:T(8,128)(2,1)} %grd_hbm.1, bf16[64,2048]{1,0:T(8,128)(2,1)} %bitcast.3, bf16[64,6144]{1,0:T(8,128)(2,1)} %bitcast.2, s32[8,32]{1,0:T(8,128)} %len_hbm.1, bf16[384,2048]{1,0:T(8,128)(2,1)} %train_hbm.1), custom_call_target="tpu_custom_call" | custom-call | flops 1000000000 | bytes 5000000 | tf_op jit(solution)/shard_map/pallas_call | solution.py:223
  12.6 0.6 %copy.8 = bf16[128,384]{1,0:T(8,128)(2,1)} copy(bf16[128,384]{1,0:T(8,128)(2,1)S(1)} %shard_map.64) | data formatting | bytes 196608

commit v4 on v3

--- a/solution.py
+++ b/solution.py
@@ -11,7 +11,7 @@
 GROUP = 4
 
 
-ORDERS = [4, 0, 2, 6, 3, 5, 1, 7], [0, 1, 2, 3, 4, 5, 6, 7]
+ORDERS = [4, 0, 2, 6, 3, 5, 1, 7], [0, 2, 1, 3, 4, 5, 6, 7]
 
 
 def peer(**axes):
@@ -27,8 +27,8 @@
 
 
 def kernel(n_dp, tok_hbm, grd_hbm, pin_hbm, pout_hbm, len_hbm, train_hbm, out_ref,
-           tok, grd, pin, pout, lens, train, part, other, xg, outer, member_ref, feats,
-           load_sem, train_sem, swap_send, swap_recv, a_send, a_recv, b_send, b_recv):
+           tok, grd, pin, pout, lens, train, part, other, xg, mine, halves, outer, member_ref, feats,
+           load_sem, train_sem, swap_send, swap_recv, a_send, a_recv, b_send, b_recv, half_send, half_recv):
     n_blocks = n_dp // 2
     group = min(GROUP, n_blocks)
     dp = lax.axis_index("dp")
@@ -36,6 +36,8 @@
     sibling = 1 - core
     owner = dp // n_blocks == core
     slot = lax.rem(dp, n_blocks)
+    top = dp >= n_dp - 2
+    whole = (dp == 0) & (core == 1)
     K, n_tok = part.shape[1:]
     n_ex = lens.shape[1]
     ff = grd.shape[1] // G_PIECES
@@ -53,6 +55,11 @@
         return carry
 
     lax.fori_loop(0, n_blocks, greet, 0, unroll=n_blocks <= 8)
+
+    @pl.when(whole)
+    def _():
+        for k in range(2):
+            pl.semaphore_signal(barrier, inc=1, **peer(dp=n_dp - 2 + k, tensor=0))
 
     loads = [
         pltpu.make_async_copy(pin_hbm, pin, load_sem.at[0]),
@@ -76,7 +83,7 @@
 
     def each_peer(act):
         def one(t):
-            @pl.when(t != dp)
+            @pl.when((t != dp) & jnp.logical_not((core == 1) & top & (t == 0)))
             def _():
                 act(pltpu.make_async_remote_copy(
                     xg.at[slot], xg.at[slot], b_send.at[t], b_recv.at[slot], **peer(dp=t)))
@@ -91,20 +98,32 @@
 
             lax.fori_loop(0, n_dp, step, 0)
 
+    def to_whole():
+        place = lax.rem(dp, 2)
+        return pltpu.make_async_remote_copy(
+            mine, halves.at[place, core], half_send, half_recv.at[place, core], **peer(dp=0, tensor=1))
+
+    def hand_half():
+        @pl.when(top)
+        def _():
+            mine[...] = part[...].astype(jnp.bfloat16)
+            to_whole().start()
+
     def hand_over(p):
         @pl.when(jnp.logical_not(owner))
         def _():
             if p == 0:
-                pl.semaphore_wait(barrier, 1)
+                pl.semaphore_wait(barrier, 1 + top.astype(jnp.int32))
             to_owner(p).start()
 
     def spread():
         @pl.when(owner)
         def _():
+            pl.semaphore_wait(barrier, n_dp)
+            hand_half()
             for p in range(2):
                 to_owner(p).wait_recv()
                 xg[slot, p] = (part[p] + other[p]).astype(jnp.bfloat16)
-            pl.semaphore_wait(barrier, n_dp)
             each_peer(lambda copy: copy.start())
 
     loads[0].wait()
@@ -121,6 +140,11 @@
             part[1] += term
     hand_over(1)
     spread()
+
+    @pl.when(jnp.logical_not(owner))
+    def _():
+        hand_half()
+
     own_train.start()
     swap.start()
 
@@ -146,7 +170,19 @@
         member_ref[...] = member
 
         def arrive(at):
-            @pl.when(jnp.logical_not(owner & (at == slot)))
+            split = whole & (at >= n_blocks - 2)
+
+            @pl.when(split)
+            def _():
+                place = lax.rem(at, 2)
+                for k in range(2):
+                    pltpu.make_async_remote_copy(
+                        halves.at[place, k], halves.at[place, k], half_send, half_recv.at[place, k],
+                        **peer(tensor=sibling)).wait_recv()
+                total = halves[place, 0].astype(jnp.float32) + halves[place, 1].astype(jnp.float32)
+                xg[at] = total.astype(jnp.bfloat16)
+
+            @pl.when(jnp.logical_not(split | (owner & (at == slot))))
             def _():
                 pltpu.make_async_remote_copy(
                     xg.at[at], xg.at[at], b_send.at[0], b_recv.at[at], **peer(tensor=sibling)).wait_recv()
@@ -199,6 +235,10 @@
         lax.fori_loop(0, n_blocks // group, step, 0)
 
     swap.wait_send()
+
+    @pl.when(top)
+    def _():
+        to_whole().wait_send()
 
     @pl.when(jnp.logical_not(owner))
     def _():
@@ -235,6 +275,8 @@
             pltpu.VMEM((2, K, n_tok), f32),
             pltpu.VMEM((2, K, n_tok), f32),
             pltpu.VMEM((n_blocks, 2, K, n_tok), bf16),
+            pltpu.VMEM((2, K, n_tok), bf16),
+            pltpu.VMEM((2, 2, 2, K, n_tok), bf16),
             pltpu.VMEM((2, K // 2 * n_ex, 2 * n_tok), bf16),
             pltpu.VMEM((group * n_ex, n_tok), bf16),
             pltpu.VMEM((group * n_ex, K * K), bf16),
@@ -246,6 +288,8 @@
             dma((2,)),
             dma((n_dp,)),
             dma((n_blocks,)),
+            dma,
+            dma((2, 2)),
         ],
         compiler_params=pltpu.CompilerParams(
             collective_id=0, has_side_effects=True, vmem_limit_bytes=40 * 1024 * 1024),

time: 13.4 us -> 13.4 us (level)
  the two profiles are of different devices: /device:TPU:1 before, /device:TPU:7 now
where the time goes in v4:
time: 13.4 us; the launch traced here: 13.2 us
  Pallas kernels  12.6 us (94%)
  local copies, waits for them, and re-layouts  0.64 us (5%)
    pallas_call x1, Pallas kernels, shards(): pl.pallas_call(functools.partial(kernel, n_dp), out_shape=jax.ShapeDtypeS...  12.6 us
    unnamed x1, local copies, waits for them, and re-layouts  0.64 us

profile of v4, /device:TPU:7, one launch (start us, length us, event | category | flops | bytes accessed | tf_op | source)
XLA Modules:
  0.0 13.2 jit_solution(6295484472895092628)
XLA Ops:
  0.0 12.6 %shard_map.64 = bf16[128,384]{1,0:T(8,128)(2,1)S(1)} custom-call(bf16[128,2048]{1,0:T(8,128)(2,1)} %tok_hbm.1, bf16[128,6144]{1,0:T(8,128)(2,1)} %grd_hbm.1, bf16[64,2048]{1,0:T(8,128)(2,1)} %bitcast.3, bf16[64,6144]{1,0:T(8,128)(2,1)} %bitcast.2, s32[8,32]{1,0:T(8,128)} %len_hbm.1, bf16[384,2048]{1,0:T(8,128)(2,1)} %train_hbm.1), custom_call_target="tpu_custom_call" | custom-call | flops 1000000000 | bytes 5000000 | tf_op jit(solution)/shard_map/pallas_call | solution.py:263
  12.6 0.6 %copy.8 = bf16[128,384]{1,0:T(8,128)(2,1)} copy(bf16[128,384]{1,0:T(8,128)(2,1)S(1)} %shard_map.64) | data formatting | bytes 196608
